TPU v7x, 32 devices: a whole 2x2x4 slice. The times are simulated.
32 devices in a mesh: src: 8 (over z, core), tgt: 4 (over y, x).
Axes of the slice: x: 2, y: 2, z: 4, core: 2. Of those that a mesh axis runs over, the one named last changes fastest.
Arguments:
- positions: float32 [3, 4096], P(None, ('src', 'tgt')), as said below
- contact_bodies: int32 [2, 32768], P(None, ('src', 'tgt')), may hold values from 0 to 4095, as said below
- contact_frame: float32 [9, 32768], P(None, ('src', 'tgt')), as said below
- gaps: float32 [32768], P(('src', 'tgt')), may hold values from -1 to 1
- impulse_now: float32 [32768], P(('src', 'tgt')), may hold values from 0 to 1
- impulse_prev: float32 [32768], P(('src', 'tgt')), may hold values from 0 to 1
- step_sizes: float32 [2], replicated, may hold values from 0.05 to 0.2
Outputs:
- impulse: float32 [32768], P(('src', 'tgt'))
- body_velocity: float32 [6, 4096], P(None, ('src', 'tgt'))
Inputs may be any that keep to these rules, and one draw needn't show every extreme that they name: `contact_bodies`: each contact joins a body i with body i + 1, i + 32 or i + 1024, modulo 4096. `positions`: body k lies within 0.45 of the point 3 (k mod 32, k // 32 mod 32, k // 1024) along each coordinate. `contact_frame`: rows 0 to 2 of each column are a unit vector; rows 3 to 8 lie in -2 to 2.
All inputs are finite; a program needn't handle non-finite values.
Results may differ from a plain program's by a relative error of at most 0.0003.
Values sent between devices are 32-bit elements; how exact they have to be, the bound alone decides.
A program may use at most 64 MiB of HBM per device.

v0:
```python
import math

import jax
import jax.numpy as jnp
from jax import lax
from jax.sharding import PartitionSpec as P

ITERS = 2


MOMENTUM = 0.4


def cross_product(first, second):
    return jnp.stack(
        [
            first[1] * second[2] - first[2] * second[1],
            first[2] * second[0] - first[0] * second[2],
            first[0] * second[1] - first[1] * second[0],
        ]
    )


def contact_rows(frame):
    normal = frame[0:3]
    lever_first = cross_product(frame[3:6], normal)
    lever_second = cross_product(frame[6:9], normal)
    return (jnp.concatenate([-normal, -lever_first]), jnp.concatenate([normal, lever_second]))


def pair_block(target_pos, target_ids, source_pos, source_ids, forces):
    delta_x = target_pos[0][:, None] - source_pos[0][None, :]
    delta_y = target_pos[1][:, None] - source_pos[1][None, :]
    delta_z = target_pos[2][:, None] - source_pos[2][None, :]
    coincide = target_ids[:, None] == source_ids[None, :]
    dist_sq = jnp.where(coincide, 1.0, delta_x * delta_x + delta_y * delta_y + delta_z * delta_z)
    inverse = jnp.where(coincide, 0.0, lax.rsqrt(dist_sq))
    self_term = jnp.where(coincide, 1.0, 0.0)
    unit_x = delta_x * inverse
    unit_y = delta_y * inverse
    unit_z = delta_z * inverse
    force_x, force_y, force_z = (forces[0][None, :], forces[1][None, :], forces[2][None, :])
    torque_x, torque_y, torque_z = (forces[3][None, :], forces[4][None, :], forces[5][None, :])
    inverse_sq = inverse * inverse
    c_one = 0.75 * inverse
    c_two = 0.75 * inverse_sq
    c_three = 0.375 * inverse_sq * inverse
    along_force = unit_x * force_x + unit_y * force_y + unit_z * force_z
    along_torque = unit_x * torque_x + unit_y * torque_y + unit_z * torque_z
    isotropic = c_one * (1.0 + inverse_sq * (2.0 / 3.0)) + self_term
    dyadic = c_one * (1.0 - 2.0 * inverse_sq) * along_force
    vel_x = isotropic * force_x + dyadic * unit_x + c_two * (torque_y * unit_z - torque_z * unit_y)
    vel_y = isotropic * force_y + dyadic * unit_y + c_two * (torque_z * unit_x - torque_x * unit_z)
    vel_z = isotropic * force_z + dyadic * unit_z + c_two * (torque_x * unit_y - torque_y * unit_x)
    spin_self = 0.75 * self_term - c_three
    spin_x = (
        c_two * (force_y * unit_z - force_z * unit_y)
        + c_three * 3.0 * unit_x * along_torque
        + spin_self * torque_x
    )
    spin_y = (
        c_two * (force_z * unit_x - force_x * unit_z)
        + c_three * 3.0 * unit_y * along_torque
        + spin_self * torque_y
    )
    spin_z = (
        c_two * (force_x * unit_y - force_y * unit_x)
        + c_three * 3.0 * unit_z * along_torque
        + spin_self * torque_z
    )
    return jnp.stack(
        [
            jnp.sum(vel_x, 1),
            jnp.sum(vel_y, 1),
            jnp.sum(vel_z, 1),
            jnp.sum(spin_x, 1),
            jnp.sum(spin_y, 1),
            jnp.sum(spin_z, 1),
        ]
    )


def assemble(slots_first, slots_second, first_rows, second_rows, shifted, body_count):
    forces = jnp.zeros((6, body_count), jnp.float32)
    forces = forces.at[:, slots_first].add(first_rows * shifted[None, :])
    return forces.at[:, slots_second].add(second_rows * shifted[None, :])


def per_device(
    positions, contact_bodies, contact_frame, gaps, impulse_now, impulse_prev, step_sizes
):
    src_count = lax.axis_size("src")
    tgt_count = lax.axis_size("tgt")
    own_rows = positions.shape[1]
    src_place = lax.axis_index("src")
    tgt_place = lax.axis_index("tgt")
    body_count = own_rows * src_count * tgt_count
    target_pos = lax.all_gather(positions, "tgt", axis=1, tiled=True)
    source_pos = lax.all_gather(positions, "src", axis=1, tiled=True)
    target_ids = src_place * tgt_count * own_rows + jnp.arange(
        tgt_count * own_rows, dtype=jnp.int32
    )
    gathered_index = jnp.arange(src_count * own_rows, dtype=jnp.int32)
    source_ids = (
        gathered_index // own_rows * tgt_count + tgt_place
    ) * own_rows + gathered_index % own_rows
    first_rows, second_rows = contact_rows(contact_frame)
    empty = jnp.zeros((6, tgt_count * own_rows), jnp.float32)
    current = impulse_now
    shifted = impulse_now + MOMENTUM * (impulse_now - impulse_prev)
    own_velocity = jnp.zeros((6, own_rows), jnp.float32)
    for k in range(ITERS):
        piece_first = contact_bodies[0] // own_rows
        piece_second = contact_bodies[1] // own_rows
        slot_first = (
            piece_first % tgt_count * src_count * own_rows
            + piece_first // tgt_count * own_rows
            + contact_bodies[0] % own_rows
        )
        slot_second = (
            piece_second % tgt_count * src_count * own_rows
            + piece_second // tgt_count * own_rows
            + contact_bodies[1] % own_rows
        )
        forces = assemble(slot_first, slot_second, first_rows, second_rows, shifted, body_count)
        column = lax.psum_scatter(forces, "tgt", scatter_dimension=1, tiled=True)
        column = lax.psum(column, "src")
        shard_piece = column
        length = shard_piece.shape[1]
        block_width = math.gcd(length, 256)
        blocks = length // block_width

        def one_block(block_index, running_sum):
            inner = block_index * block_width
            force_block = lax.dynamic_slice_in_dim(shard_piece, inner, block_width, 1)
            place_block = lax.dynamic_slice_in_dim(source_pos, 0 + inner, block_width, 1)
            ids_block = lax.dynamic_slice_in_dim(source_ids, 0 + inner, block_width, 0)
            return running_sum + pair_block(
                target_pos, target_ids, place_block, ids_block, force_block
            )

        partial_value = lax.fori_loop(0, blocks, one_block, empty)
        own_velocity = lax.psum_scatter(partial_value, "tgt", scatter_dimension=1, tiled=True)
        gathered = lax.all_gather(own_velocity, ("src", "tgt"), axis=1, tiled=True)
        normal_rate = jnp.sum(first_rows * gathered[:, contact_bodies[0]], 0) + jnp.sum(
            second_rows * gathered[:, contact_bodies[1]], 0
        )
        updated = jnp.maximum(shifted - step_sizes[k] * (gaps + normal_rate), 0.0)
        shifted = updated + MOMENTUM * (updated - current)
        current = updated
    return (current, own_velocity)


def solution(mesh):
    placed = (
        P(None, ("src", "tgt")),
        P(None, ("src", "tgt")),
        P(None, ("src", "tgt")),
        P(("src", "tgt")),
        P(("src", "tgt")),
        P(("src", "tgt")),
        P(),
    )
    return jax.shard_map(
        per_device,
        mesh=mesh,
        in_specs=placed,
        out_specs=(P(("src", "tgt")), P(None, ("src", "tgt"))),
        check_vma=False,
    )
```

profile of v0, /device:TPU:0, one launch (start us, length us, event | category | flops | bytes accessed | tf_op | source)
XLA Modules:
  0.0 443.8 jit_solution(13981809881268094989)
XLA Ops:
  7.2 1.1 multiply_subtract_fusion.2
  8.3 1.0 multiply_subtract_fusion.1
  9.3 0.7 multiply_add_fusion.3
  10.0 0.8 fusion.45
  10.8 0.2 copy.64
  11.1 0.9 compare_select_fusion.8
  12.0 0.2 copy.65
  12.2 6.5 %scatter_custom_fusion = f32[6,4096]{0,1:T(8,128)S(1)} fusion(s32[1024]{0:T(1024)S(1)} %bitcast.210, f32[1024,6]{1,0:T(8,128)S(1)} %copy.64, f32[]{:T(128)} %constant.262.clone.1), kind=kCustom, calls=%fused_computation.72 | custom fusion | flops 6144 | bytes 98308 | tf_op jit(solution)/shard_map/scatter-add | solution.py:85
  18.8 6.8 %scatter_fusion = f32[6,4096]{0,1:T(8,128)S(1)} fusion(f32[6,4096]{0,1:T(8,128)S(1)} %scatter_custom_fusion, s32[1024]{0:T(1024)S(1)} %bitcast.188, f32[1024,6]{1,0:T(8,128)S(1)} %copy.65), kind=kCustom, calls=%fused_computation.5 | custom fusion | flops 6144 | bytes 77824 | tf_op jit(solution)/shard_map/scatter-add | solution.py:86
  25.6 1.3 copy-done.1
  27.0 14.4 %all_gather.13 = f32[3,1024]{1,0:T(4,128)S(1)} all-gather(f32[3,128]{1,0:T(4,128)S(1)} %copy-done.6), channel_id=1, replica_groups=mesh['src'=8,'tgt'=4] {'src'}, dimensions={1}, use_global_device_ids=true | all-gather | bytes 13824 | tf_op jit(solution)/shard_map/all_gather | solution.py:99
  41.4 8.1 %all_gather.12 = f32[3,512]{1,0:T(4,128)S(1)} all-gather(f32[3,128]{1,0:T(4,128)S(1)} %copy-done.6), channel_id=1, replica_groups=mesh['src'=8,'tgt'=4] {'tgt'}, dimensions={1}, use_global_device_ids=true | all-gather | bytes 7680 | tf_op jit(solution)/shard_map/all_gather | solution.py:98
  49.5 15.5 %reduce-scatter.5.cloned.1.call-done = f32[6,1024]{0,1:T(8,128)} async-done(((f32[6,4096]{0,1:T(8,128)}), f32[6,1024]{0,1:T(8,128)}) %reduce-scatter.5.cloned.1.call-update) | async-done | bytes 24592 | tf_op jit(solution)/shard_map/reduce_scatter | solution.py:126
  65.0 35.9 %psum.14 = f32[6,1024]{0,1:T(8,128)S(1)} all-reduce(f32[6,1024]{0,1:T(8,128)} %reduce-scatter.5.cloned.1.call-done), channel_id=1, replica_groups=mesh['src'=8,'tgt'=4] {'src'}, use_global_device_ids=true, to_apply=%region_3.4 | all-reduce | flops 6144 | bytes 49152 | tf_op jit(solution)/shard_map/psum | solution.py:127
  100.9 0.2 copy.66
  101.1 12.5 %while.28 = (s32[]{:T(128)}, f32[6,512]{1,0:T(8,128)S(1)}, s32[1024]{0:T(1024)S(1)}, f32[3,512]{1,0:T(4,128)S(1)}, f32[3,1024]{1,0:T(4,128)S(1)}, /*index=5*/f32...) while((s32[]{:T(128)}, f32[6,512]{1,0:T(8,128)S(1)}, ...), condition=%wide.region_11.12_spmd.clone, body=%wide.region_4.11_spmd.clone.sunk | while | flops 12848652 | bytes 127273 | solution.py:142
  101.1 0.1 constant_dynamic-slice_fusion.6
  101.2 0.1 dynamic_slice.50
  101.3 2.9 add_reduce_fusion.14
  104.2 0.1 constant_dynamic-slice_fusion.6
  104.4 2.9 add_reduce_fusion.14
  107.4 0.1 constant_dynamic-slice_fusion.6
  107.6 2.9 add_reduce_fusion.14
  110.5 0.1 constant_dynamic-slice_fusion.6
  110.7 2.9 add_reduce_fusion.14
  113.7 0.8 copy.67
  114.6 0.6 fusion.46
  115.2 0.2 copy.69
  115.4 0.2 copy.68
  115.7 20.3 %reduce-scatter.7.cloned.1.call-done = f32[6,128]{0,1:T(8,128)} async-done(((f32[6,512]{0,1:T(8,128)}), f32[6,128]{0,1:T(8,128)}) %reduce-scatter.7.cloned.1.call-update) | async-done | bytes 3088 | tf_op jit(solution)/shard_map/reduce_scatter | solution.py:143
  136.0 78.6 %all_gather.14 = f32[6,4096]{0,1:T(8,128)S(1)} all-gather(f32[6,128]{0,1:T(8,128)} %reduce-scatter.7.cloned.1.call-done), channel_id=1, replica_groups=mesh['src'=8,'tgt'=4] {'src','tgt'}, dimensions={1}, use_global_device_ids=true | all-gather | bytes 101376 | tf_op jit(solution)/shard_map/all_gather | solution.py:144
  214.6 4.0 gather_fusion.1
  218.6 4.0 gather_fusion
  222.6 1.3 fusion.22
  223.8 1.3 fusion.23
  225.1 0.7 multiply_add_fusion.2
  225.9 1.0 copy.70
  226.9 6.9 %scatter_custom_fusion.2 = f32[6,4096]{0,1:T(8,128)S(1)} fusion(s32[1024]{0:T(1024)S(1)} %bitcast.211, f32[1024,6]{1,0:T(8,128)} %copy.70, f32[]{:T(128)} %constant.262.clone.1), kind=kCustom, calls=%fused_computation.70 | custom fusion | flops 6144 | bytes 98816 | tf_op jit(solution)/shard_map/scatter-add | solution.py:85
  233.8 1.0 copy.71
  234.8 7.4 %scatter_fusion.1 = f32[6,4096]{0,1:T(8,128)S(1)} fusion(f32[6,4096]{0,1:T(8,128)S(1)} %scatter_custom_fusion.2, s32[1024]{0:T(1024)S(1)} %bitcast.189, f32[1024,6]{1,0:T(8,128)} %copy.71), kind=kCustom, calls=%fused_computation.7 | custom fusion | flops 6144 | bytes 77824 | tf_op jit(solution)/shard_map/scatter-add | solution.py:86
  242.2 1.3 copy-done
  243.7 31.5 %reduce-scatter.9.cloned.1.call-done = f32[6,1024]{0,1:T(8,128)} async-done(((f32[6,4096]{0,1:T(8,128)}), f32[6,1024]{0,1:T(8,128)}) %reduce-scatter.9.cloned.1.call-update) | async-done | bytes 24592 | tf_op jit(solution)/shard_map/reduce_scatter | solution.py:126
  275.2 35.9 %psum.15 = f32[6,1024]{0,1:T(8,128)S(1)} all-reduce(f32[6,1024]{0,1:T(8,128)} %reduce-scatter.9.cloned.1.call-done), channel_id=1, replica_groups=mesh['src'=8,'tgt'=4] {'src'}, use_global_device_ids=true, to_apply=%region_18.19 | all-reduce | flops 6144 | bytes 49152 | tf_op jit(solution)/shard_map/psum | solution.py:127
  311.0 0.2 copy.72
  311.2 12.5 %while.29 = (s32[]{:T(128)}, f32[6,512]{1,0:T(8,128)S(1)}, s32[1024]{0:T(1024)S(1)}, f32[3,512]{1,0:T(4,128)S(1)}, f32[3,1024]{1,0:T(4,128)S(1)}, /*index=5*/f32...) while((s32[]{:T(128)}, f32[6,512]{1,0:T(8,128)S(1)}, ...), condition=%wide.region_26.27_spmd.clone, body=%wide.region_19.26_spmd.clone.sunk | while | flops 12848652 | bytes 127273 | solution.py:142
  311.2 0.1 constant_dynamic-slice_fusion.7
  311.3 0.1 dynamic_slice.51
  311.4 2.9 add_reduce_fusion.15
  314.4 0.1 constant_dynamic-slice_fusion.7
  314.5 0.1 dynamic_slice.51
  314.6 2.9 add_reduce_fusion.15
  317.5 0.1 constant_dynamic-slice_fusion.7
  317.7 2.9 add_reduce_fusion.15
  320.7 0.1 constant_dynamic-slice_fusion.7
  320.8 2.9 add_reduce_fusion.15
  323.8 0.8 copy.73
  324.7 21.4 %reduce-scatter.11.cloned.1.call-done = f32[6,128]{0,1:T(8,128)} async-done(((f32[6,512]{0,1:T(8,128)}), f32[6,128]{0,1:T(8,128)}) %reduce-scatter.11.cloned.1.call-update) | async-done | bytes 3088 | tf_op jit(solution)/shard_map/reduce_scatter | solution.py:143
  346.1 78.7 %all_gather.15 = f32[6,4096]{0,1:T(8,128)S(1)} all-gather(f32[6,128]{0,1:T(8,128)} %reduce-scatter.11.cloned.1.call-done), channel_id=1, replica_groups=mesh['src'=8,'tgt'=4] {'src','tgt'}, dimensions={1}, use_global_device_ids=true | all-gather | bytes 101376 | tf_op jit(solution)/shard_map/all_gather | solution.py:144
  424.8 4.0 gather_fusion.3
  428.8 4.0 gather_fusion.2
  432.8 1.3 fusion.20
  434.1 1.3 fusion.21
  435.3 1.2 subtract_maximum_fusion
  436.6 0.7 copy.76
  (66 shorter events, 1.1 us)
Async XLA Ops:
  7.2 57.9 %reduce-scatter.5.cloned.1.call-start = ((), (), s32[]{:S(2)}) async-start(), calls=%async_computation.4 | async-start | bytes 2621440 | tf_op jit(solution)/shard_map/reduce_scatter | solution.py:126
  12.2 14.8 %copy-start.6 = (f32[3,128]{1,0:T(4,128)S(1)}, f32[3,128]{1,0:T(4,128)}, u32[]{:S(2)}) copy-start(f32[3,128]{1,0:T(4,128)} %param.11) | copy-start | bytes 4612
  25.6 1.4 copy-start.1
  26.9 109.1 %reduce-scatter.7.cloned.1.call-start = ((), (), s32[]{:S(2)}) async-start(), calls=%async_computation.5 | async-start | bytes 327680 | tf_op jit(solution)/shard_map/reduce_scatter | solution.py:143
  100.9 13.7 %copy-start.7 = (f32[2]{0:T(128)S(1)}, f32[2]{0:T(128)}, u32[]{:S(2)}) copy-start(f32[2]{0:T(128)} %param.17) | copy-start | bytes 28
  114.5 160.6 %reduce-scatter.9.cloned.1.call-start = ((), (), s32[]{:S(2)}) async-start(), calls=%async_computation.6 | async-start | bytes 2621440 | tf_op jit(solution)/shard_map/reduce_scatter | solution.py:126
  115.6 109.5 %copy-start.3 = (f32[1024]{0:T(1024)S(1)}, f32[1024]{0:T(1024)}, u32[]{:S(2)}) copy-start(f32[1024]{0:T(1024)} %param.15) | copy-start | bytes 12292
  115.7 109.5 %copy-start.4 = (f32[1024]{0:T(1024)S(1)}, f32[1024]{0:T(1024)}, u32[]{:S(2)}) copy-start(f32[1024]{0:T(1024)} %param.16) | copy-start | bytes 12292
  115.7 109.5 %copy-start.5 = (f32[1024]{0:T(1024)S(1)}, f32[1024]{0:T(1024)}, u32[]{:S(2)}) copy-start(f32[1024]{0:T(1024)} %param.14) | copy-start | bytes 12292
  242.2 1.4 copy-start
  243.6 102.5 %reduce-scatter.11.cloned.1.call-start = ((), (), s32[]{:S(2)}) async-start(), calls=%async_computation.7 | async-start | bytes 327680 | tf_op jit(solution)/shard_map/reduce_scatter | solution.py:143
  346.1 90.5 %copy-start.2 = (f32[6,128]{0,1:T(8,128)S(1)}, f32[6,128]{0,1:T(8,128)}, u32[]{:S(2)}) copy-start(f32[6,128]{0,1:T(8,128)} %reduce-scatter.11.cloned.1.call-done) | copy-start | bytes 9220
Sparse Core Ops, SparseCore 0:
  27.1 37.9 reduce-scatter.4
  114.6 21.3 reduce-scatter.6
  243.7 31.4 reduce-scatter.8
  324.8 21.2 reduce-scatter.10
where the time goes:
time: 445 us; the launch traced here: 444 us
  blocking collectives  251 us (56%)
  waiting for transfers between devices  88.9 us (20%)
  other arithmetic  62.3 us (14%)
  local copies, waits for them, and re-layouts  26.7 us (6%)
  between operations  14.1 us (3%)
    all_gather x2, blocking collectives, per_device(): gathered = lax.all_gather(own_velocity, ('src', 'tgt'), axis=1, tiled=True)  157 us
    psum x2, blocking collectives, per_device(): column = lax.psum(column, 'src')  71.7 us
    reduce_scatter x2, waiting for transfers between devices, per_device(): column = lax.psum_scatter(forces, 'tgt', scatter_dimension=1, tiled=True)  47 us
    reduce_scatter x2, waiting for transfers between devices, per_device(): lax.psum_scatter(partial_value, 'tgt', scatter_dimension=1, tiled=True)  41.8 us
    reduce_sum x8, other arithmetic, pair_block(): jnp.sum(spin_z, 1)  23 us
    all_gather x1, blocking collectives, per_device(): source_pos = lax.all_gather(positions, 'src', axis=1, tiled=True)  14.4 us
    scatter-add x2, other arithmetic, assemble(): return forces.at[:, slots_second].add(second_rows * shifted[None, :])  14.2 us
    scatter-add x2, other arithmetic, assemble(): forces = forces.at[:, slots_first].add(first_rows * shifted[None, :])  13.4 us
  transfers between devices with their start and end apart: 4, of which 4 were waited for; matrix products, arithmetic and copies ran while one was open for 0% of the time, Pallas kernels for 0%

commit v1 on v0

v1 whole, which is shorter than its diff:
```python
import functools

import jax
import jax.numpy as jnp
from jax import lax
from jax.experimental import pallas as pl
from jax.experimental.pallas import tpu as pltpu
from jax.sharding import PartitionSpec as P

ITERS = 2
MOMENTUM = 0.4
GROUP = 16

F32 = jnp.float32
BF16 = jnp.bfloat16


def halves(value):
    high = value.astype(BF16)
    return high, (value - high.astype(F32)).astype(BF16)


def cross_rows(first, second):
    return [
        first[1] * second[2] - first[2] * second[1],
        first[2] * second[0] - first[0] * second[2],
        first[0] * second[1] - first[1] * second[0],
    ]


def kernel(
    src_count,
    tgt_count,
    pos_ref,
    bodies_ref,
    frame_ref,
    gaps_ref,
    now_ref,
    prev_ref,
    step_ref,
    impulse_ref,
    velocity_ref,
    pos_all,
    part,
    arrived,
    force_all,
    vel_all,
    target_pos,
    coef,
    total,
    spread,
    onehot,
    picked,
    send_sem,
    recv_sem,
):
    n = src_count * tgt_count
    lanes = pos_ref.shape[1]
    contacts = gaps_ref.shape[1]
    me = lax.axis_index("src") * tgt_count + lax.axis_index("tgt")

    def place(device):
        return (device // tgt_count, lax.rem(device, tgt_count))

    def send_all(source, landing, phase):
        def one(k, carry):
            device = lax.rem(me + k, n)
            pltpu.make_async_remote_copy(
                src_ref=source(device),
                dst_ref=landing.at[me],
                send_sem=send_sem.at[phase],
                recv_sem=recv_sem.at[phase],
                device_id=place(device),
                device_id_type=pl.DeviceIdType.MESH,
            ).start()
            return carry

        lax.fori_loop(1, n, one, 0)

    def wait_all(landing, sem):
        blocks = landing.at[pl.ds(0, n - 1)]
        pltpu.make_async_copy(blocks, blocks, sem).wait()

    barrier = pltpu.get_barrier_semaphore()

    def greet(k, carry):
        pl.semaphore_signal(
            barrier,
            inc=1,
            device_id=place(lax.rem(me + k, n)),
            device_id_type=pl.DeviceIdType.MESH,
        )
        return carry

    lax.fori_loop(1, n, greet, 0)

    normal = [frame_ref[r : r + 1, :] for r in range(3)]
    arm_first = [frame_ref[r : r + 1, :] for r in range(3, 6)]
    arm_second = [frame_ref[r : r + 1, :] for r in range(6, 9)]
    empty = jnp.zeros((1, contacts), F32)
    second_rows = jnp.concatenate(normal + cross_rows(arm_second, normal) + [empty, empty], 0)
    first_rows = -jnp.concatenate(normal + cross_rows(arm_first, normal) + [empty, empty], 0)
    rows = [first_rows, second_rows]

    lane_ids = lax.broadcasted_iota(jnp.int32, (lanes, contacts), 0)
    pair_half = lax.broadcasted_iota(jnp.int32, (16, contacts), 0) // 8
    block_ids = []
    for end in range(2):
        body = bodies_ref[end : end + 1, :]
        block = body // lanes
        block_ids.append(block - pair_half)
        hot = jnp.where(lane_ids == body - block * lanes, 1.0, 0.0).astype(BF16)
        onehot[0:lanes, end * contacts : (end + 1) * contacts] = hot
        onehot[lanes : 2 * lanes, end * contacts : (end + 1) * contacts] = hot

    pos_own = jnp.concatenate([pos_ref[...], jnp.zeros((5, lanes), F32)], 0)
    pos_all[me] = pos_own
    for r in range(3):
        target_pos[r] = jnp.broadcast_to(pos_own[r : r + 1, :], (lanes, lanes)).T

    pl.semaphore_wait(barrier, n - 1)
    send_all(lambda device: pos_all.at[me], pos_all, 0)

    current = now_ref[...]
    shifted = current + MOMENTUM * (current - prev_ref[...])

    for k in range(ITERS):
        pieces = []
        for end in range(2):
            value = rows[end] * shifted
            high = value.astype(BF16).astype(F32)
            low = value - high
            pieces.append(
                (jnp.concatenate([high, high], 0), jnp.concatenate([low, low], 0))
            )

        def lay_out(step, carry):
            inner = pl.multiple_of(step * 16, 16)
            for end in range(2):
                here = block_ids[end] == 2 * step
                for half in range(2):
                    spread[
                        half, pl.ds(inner, 16), end * contacts : (end + 1) * contacts
                    ] = jnp.where(here, pieces[end][half], 0.0).astype(BF16)
            return carry

        lax.fori_loop(0, n // 2, lay_out, 0)
        both = lax.dot_general(
            spread[...].reshape(2 * n * 8, 2 * contacts),
            onehot[0:lanes, :],
            (((1,), (1,)), ((), ())),
            preferred_element_type=F32,
        )
        part[k] = (both[: n * 8] + both[n * 8 :]).reshape(n, 8, lanes)
        arrived[k, me] = part[k, me]
        send_all(lambda device: part.at[k, device], arrived.at[k], 1 + 3 * k)

        if k == 0:
            wait_all(pos_all, recv_sem.at[0])

            def coefficients(step, carry):
                block = step // (lanes // GROUP)
                group = pl.ds(
                    pl.multiple_of(lax.rem(step, lanes // GROUP) * GROUP, GROUP), GROUP
                )
                dist_sq = None
                for r in range(3):
                    delta = target_pos[r, group, :] - pos_all[block, r : r + 1, :]
                    dist_sq = delta * delta if r == 0 else dist_sq + delta * delta
                inverse = lax.rsqrt(dist_sq)
                inverse_sq = inverse * inverse
                c_one = 0.75 * inverse
                gamma = c_one * inverse_sq
                scaled = gamma * inverse_sq
                coef[block, 0, group, :] = c_one + gamma * (2.0 / 3.0)
                coef[block, 1, group, :] = gamma - 2.0 * scaled
                coef[block, 2, group, :] = gamma
                coef[block, 3, group, :] = 1.5 * scaled
                return carry

            lax.fori_loop(0, n * (lanes // GROUP), coefficients, 0, unroll=2)
            diagonal = lax.broadcasted_iota(
                jnp.int32, (lanes, lanes), 0
            ) == lax.broadcasted_iota(jnp.int32, (lanes, lanes), 1)
            for c in range(4):
                coef[me, c] = jnp.where(diagonal, 0.0, coef[me, c])

        wait_all(arrived.at[k], recv_sem.at[1 + 3 * k])
        own_force = jnp.sum(arrived[k], 0)
        force_all[k, me] = own_force
        send_all(lambda device: force_all.at[k, me], force_all.at[k], 2 + 3 * k)
        wait_all(force_all.at[k], recv_sem.at[2 + 3 * k])

        def target_group(step, carry):
            group = pl.ds(pl.multiple_of(step * GROUP, GROUP), GROUP)
            where = [target_pos[r, group, :] for r in range(3)]

            def source_block(block, sums):
                x, y, z = [where[r] - pos_all[block, r : r + 1, :] for r in range(3)]
                f_x, f_y, f_z, t_x, t_y, t_z = [
                    force_all[k, block, r : r + 1, :] for r in range(6)
                ]
                alpha, beta, gamma, delta = [coef[block, c, group, :] for c in range(4)]
                along_force = beta * (x * f_x + y * f_y + z * f_z)
                along_torque = delta * (x * t_x + y * t_y + z * t_z)
                return (
                    sums[0] + (alpha * f_x + along_force * x + gamma * (t_y * z - t_z * y)),
                    sums[1] + (alpha * f_y + along_force * y + gamma * (t_z * x - t_x * z)),
                    sums[2] + (alpha * f_z + along_force * z + gamma * (t_x * y - t_y * x)),
                    sums[3] + (along_torque * x + gamma * (f_y * z - f_z * y - 0.5 * t_x)),
                    sums[4] + (along_torque * y + gamma * (f_z * x - f_x * z - 0.5 * t_y)),
                    sums[5] + (along_torque * z + gamma * (f_x * y - f_y * x - 0.5 * t_z)),
                )

            zero = jnp.zeros((GROUP, lanes), F32)
            sums = lax.fori_loop(0, n, source_block, (zero,) * 6, unroll=2)
            for r in range(6):
                total[r, group, :] = sums[r]
            return carry

        lax.fori_loop(0, lanes // GROUP, target_group, 0)
        own_velocity = jnp.concatenate(
            [jnp.sum(total[r].T, 0, keepdims=True) for r in range(6)]
            + [jnp.zeros((2, lanes), F32)],
            0,
        )
        row_ids = lax.broadcasted_iota(jnp.int32, (8, lanes), 0)
        own_velocity = own_velocity + jnp.where(row_ids < 3, 1.0, 0.75) * own_force
        vel_all[k, me] = own_velocity
        send_all(lambda device: vel_all.at[k, me], vel_all.at[k], 3 + 3 * k)
        if k == ITERS - 1:
            velocity_ref[...] = own_velocity[0:6]
        wait_all(vel_all.at[k], recv_sem.at[3 + 3 * k])

        high, low = halves(vel_all[k].reshape(n * 8, lanes))
        picked[...] = jnp.dot(
            jnp.concatenate([high, low], 1), onehot[...], preferred_element_type=F32
        )

        def pick(step, sums):
            inner = pl.multiple_of(step * 16, 16)
            return tuple(
                sums[end]
                + jnp.where(
                    block_ids[end] == 2 * step,
                    picked[pl.ds(inner, 16), end * contacts : (end + 1) * contacts],
                    0.0,
                )
                for end in range(2)
            )

        zero = jnp.zeros((16, contacts), F32)
        ends = lax.fori_loop(0, n // 2, pick, (zero, zero))
        rate = sum(rows[end] * (ends[end][0:8] + ends[end][8:16]) for end in range(2))
        normal_rate = jnp.sum(rate, 0, keepdims=True)
        updated = jnp.maximum(shifted - step_ref[k] * (gaps_ref[...] + normal_rate), 0.0)
        shifted = updated + MOMENTUM * (updated - current)
        current = updated

    impulse_ref[...] = current
    for phase in range(1 + 3 * ITERS):
        wait_all(pos_all, send_sem.at[phase])


def per_device(
    positions, contact_bodies, contact_frame, gaps, impulse_now, impulse_prev, step_sizes
):
    src_count = lax.axis_size("src")
    tgt_count = lax.axis_size("tgt")
    n = src_count * tgt_count
    lanes = positions.shape[1]
    contacts = gaps.shape[0]
    vmem = pl.BlockSpec(memory_space=pltpu.VMEM)
    impulse, velocity = pl.pallas_call(
        functools.partial(kernel, src_count, tgt_count),
        out_shape=(
            jax.ShapeDtypeStruct((1, contacts), F32),
            jax.ShapeDtypeStruct((6, lanes), F32),
        ),
        in_specs=[vmem] * 6 + [pl.BlockSpec(memory_space=pltpu.SMEM)],
        out_specs=(vmem, vmem),
        scratch_shapes=[
            pltpu.VMEM((n, 8, lanes), F32),
            pltpu.VMEM((ITERS, n, 8, lanes), F32),
            pltpu.VMEM((ITERS, n, 8, lanes), F32),
            pltpu.VMEM((ITERS, n, 8, lanes), F32),
            pltpu.VMEM((ITERS, n, 8, lanes), F32),
            pltpu.VMEM((3, lanes, lanes), F32),
            pltpu.VMEM((n, 4, lanes, lanes), F32),
            pltpu.VMEM((6, lanes, lanes), F32),
            pltpu.VMEM((2, n * 8, 2 * contacts), BF16),
            pltpu.VMEM((2 * lanes, 2 * contacts), BF16),
            pltpu.VMEM((n * 8, 2 * contacts), F32),
            pltpu.SemaphoreType.DMA((1 + 3 * ITERS,)),
            pltpu.SemaphoreType.DMA((1 + 3 * ITERS,)),
        ],
        compiler_params=pltpu.CompilerParams(
            collective_id=0, has_side_effects=True, vmem_limit_bytes=60 * 1024 * 1024
        ),
    )(
        positions,
        contact_bodies,
        contact_frame,
        gaps.reshape(1, contacts),
        impulse_now.reshape(1, contacts),
        impulse_prev.reshape(1, contacts),
        step_sizes,
    )
    return impulse.reshape(contacts), velocity


def solution(mesh):
    placed = (
        P(None, ("src", "tgt")),
        P(None, ("src", "tgt")),
        P(None, ("src", "tgt")),
        P(("src", "tgt")),
        P(("src", "tgt")),
        P(("src", "tgt")),
        P(),
    )
    return jax.shard_map(
        per_device,
        mesh=mesh,
        in_specs=placed,
        out_specs=(P(("src", "tgt")), P(None, ("src", "tgt"))),
        check_vma=False,
    )
```

time: 445 us -> 63.2 us (0.14)
  blocking collectives: 251 us -> 0 us
  waiting for transfers between devices: 88.9 us -> 0 us
  other arithmetic: 62.3 us -> 0 us
  Pallas kernels: 0 us -> 60.4 us
  local copies, waits for them, and re-layouts: 26.7 us -> 1.94 us
  between operations: 14.1 us -> 0.65 us
    all_gather x4 -> x0, blocking collectives: 180 us -> none  [the longest x2 157 us: per_device(): gathered = lax.all_gather(own_velocity, ('src', 'tgt'), axis=1, tiled=True)]
    reduce_scatter x4 -> x0, waiting for transfers between devices: 88.8 us -> none  [the longest x2 47 us: per_device(): column = lax.psum_scatter(forces, 'tgt', scatter_dimension=1, tiled=True)]
    psum x2 -> x0, blocking collectives: 71.7 us -> none  [per_device(): column = lax.psum(column, 'src')]
    pallas_call x0 -> x1, Pallas kernels: none -> 60.4 us  [per_device(): pl.pallas_call(functools.partial(kernel, src_count, tgt_count), out_shape...]
    reduce_sum x12 -> x0, other arithmetic: 28 us -> none  [the longest x8 23 us: pair_block(): jnp.sum(spin_z, 1)]
    scatter-add x4 -> x0, other arithmetic: 27.6 us -> none  [the longest x2 14.2 us: assemble(): return forces.at[:, slots_second].add(second_rows * shifted[None, :])]
    gather x4 -> x0, local copies, waits for them, and re-layouts: 16 us -> none  [the longest x2 8 us: per_device(): gathered[:, contact_bodies[1]]]
  transfers between devices with their start and end apart: 4 -> 0, of which waited for: 4 -> 0; matrix products, arithmetic and copies ran while one was open for 0% -> 0% of each run, Pallas kernels for 0% -> 0%
where the time goes in v1:
time: 63.2 us; the launch traced here: 63 us
  Pallas kernels  60.4 us (96%)
  local copies, waits for them, and re-layouts  1.94 us (3%)
  between operations  0.65 us (1%)
    pallas_call x1, Pallas kernels, per_device(): pl.pallas_call(functools.partial(kernel, src_count, tgt_count), out_shape...  60.4 us
    unnamed x6, local copies, waits for them, and re-layouts  1.94 us

profile of v1, /device:TPU:0, one launch (start us, length us, event | category | flops | bytes accessed | tf_op | source)
XLA Modules:
  0.0 63.0 jit_solution(617920375767720198)
XLA Ops:
  0.6 60.4 %shard_map.86 = (f32[1,1024]{1,0:T(1,128)}, f32[6,128]{1,0:T(8,128)}) custom-call(f32[3,128]{1,0:T(4,128)} %pos_ref.1, s32[2,1024]{1,0:T(2,128)} %bodies_ref.1, f32[9,1024]{1,0:T(8,128)} %frame_ref.1, f32[1,1024]{1,0:T(1,128)} %bitcast.4, f32[1,1024]{1,0:T(1,128)} %bitcast.5, f32[1,1024]{1,0:T(1,128)} %bitcast.6, f32[2]{0:T(128)} %step_ref.1), custom_call_target="tpu_custom_call" | custom-call | tf_op jit(solution)/shard_map/pallas_call | solution.py:274
  61.0 0.0 copy-start.1
  61.0 0.7 %copy-done.1 = f32[1,1024]{1,0:T(1,128)S(1)} copy-done((f32[1,1024]{1,0:T(1,128)S(1)}, f32[1,1024]{1,0:T(1,128)}, u32[]{:S(2)}) %copy-start.1) | copy-done | bytes 4120
  61.7 0.0 copy-start
  61.7 0.6 copy.11
  62.3 0.1 copy-done
  62.4 0.6 copy.12
Async XLA Ops:
  61.0 0.7 %copy-start.1 = (f32[1,1024]{1,0:T(1,128)S(1)}, f32[1,1024]{1,0:T(1,128)}, u32[]{:S(2)}) copy-start(f32[1,1024]{1,0:T(1,128)} %get-tuple-element.4) | copy-start | bytes 12292
  61.7 0.7 %copy-start = (f32[6,128]{1,0:T(8,128)S(1)}, f32[6,128]{1,0:T(8,128)}, u32[]{:S(2)}) copy-start(f32[6,128]{1,0:T(8,128)} %get-tuple-element.9) | copy-start | bytes 9220

commit v2 on v1

v2 whole, which is shorter than its diff:
```python
import functools

import jax
import jax.numpy as jnp
from jax import lax
from jax.experimental import pallas as pl
from jax.experimental.pallas import tpu as pltpu
from jax.sharding import PartitionSpec as P

ITERS = 2
MOMENTUM = 0.4
GROUP = 16

F32 = jnp.float32
BF16 = jnp.bfloat16


def halves(value):
    high = value.astype(BF16)
    return high, (value - high.astype(F32)).astype(BF16)


def cross_rows(first, second):
    return [
        first[1] * second[2] - first[2] * second[1],
        first[2] * second[0] - first[0] * second[2],
        first[0] * second[1] - first[1] * second[0],
    ]


def kernel(
    src_count,
    tgt_count,
    pos_ref,
    bodies_ref,
    frame_ref,
    gaps_ref,
    now_ref,
    prev_ref,
    step_ref,
    result_ref,
    pos_all,
    part,
    from_twin,
    summed,
    arrived,
    force_all,
    vel_all,
    target_pos,
    coef,
    total,
    spread,
    onehot,
    picked,
    send_sem,
    recv_sem,
):
    planes = src_count // 2
    chips = planes * tgt_count
    lanes = pos_ref.shape[1]
    contacts = gaps_ref.shape[1]
    src = lax.axis_index("src")
    tgt = lax.axis_index("tgt")
    core = lax.rem(src, 2)
    plane = src // 2
    me = src * tgt_count + tgt
    twin = (src + 1 - 2 * core, tgt)

    def for_peers(visit):
        def one_plane(i, carry):
            there = lax.rem(plane + i, planes)
            for j in range(tgt_count):
                visit(there, lax.rem(tgt + j, tgt_count))
            return carry

        for j in range(1, tgt_count):
            visit(plane, lax.rem(tgt + j, tgt_count))
        lax.fori_loop(1, planes, one_plane, 0)

    def start_copy(source, landing, phase, slot, device, to_twin=0):
        pltpu.make_async_remote_copy(
            src_ref=source,
            dst_ref=landing,
            send_sem=send_sem.at[phase, to_twin],
            recv_sem=recv_sem.at[phase, slot],
            device_id=device,
            device_id_type=pl.DeviceIdType.MESH,
        ).start()

    def wait_for(blocks, sem):
        pltpu.make_async_copy(blocks, blocks, sem).wait()

    def chunk(buffer, group):
        return buffer.at[pl.ds(group * tgt_count, tgt_count)]

    def gather_start(buffer, phase, height):
        block = buffer.at[me, pl.ds(0, height)]
        for_peers(
            lambda there, column: start_copy(
                block, block, phase, src, (2 * there + core, column)
            )
        )

    def gather_own(buffer, phase, height, i):
        group = 2 * lax.rem(plane + i, planes) + core
        count = tgt_count - 1 if isinstance(i, int) and i == 0 else tgt_count
        wait_for(
            buffer.at[pl.ds(group * tgt_count, count), pl.ds(0, height)],
            recv_sem.at[phase, group],
        )
        blocks = chunk(buffer, group)
        start_copy(blocks, blocks, phase, group, twin, 1)
        return group

    def gather_twin(buffer, phase, i):
        group = 2 * lax.rem(plane + i, planes) + 1 - core
        wait_for(chunk(buffer, group), recv_sem.at[phase, group])
        return group

    def gather_sent(buffer, phase, height):
        wait_for(buffer.at[pl.ds(0, chips - 1), pl.ds(0, height)], send_sem.at[phase, 0])
        wait_for(buffer.at[pl.ds(0, chips)], send_sem.at[phase, 1])

    pos_all[...] = jnp.zeros_like(pos_all)
    force_all[...] = jnp.zeros_like(force_all)
    vel_all[...] = jnp.zeros_like(vel_all)

    barrier = pltpu.get_barrier_semaphore()

    def greet(device):
        pl.semaphore_signal(
            barrier, inc=1, device_id=device, device_id_type=pl.DeviceIdType.MESH
        )

    greet(twin)
    for_peers(lambda there, column: greet((2 * there + core, column)))

    normal = [frame_ref[r : r + 1, :] for r in range(3)]
    arm_first = [frame_ref[r : r + 1, :] for r in range(3, 6)]
    arm_second = [frame_ref[r : r + 1, :] for r in range(6, 9)]
    empty = jnp.zeros((1, contacts), F32)
    second_rows = jnp.concatenate(normal + cross_rows(arm_second, normal) + [empty, empty], 0)
    first_rows = -jnp.concatenate(normal + cross_rows(arm_first, normal) + [empty, empty], 0)
    rows = [first_rows, second_rows]

    lane_ids = lax.broadcasted_iota(jnp.int32, (lanes, contacts), 0)
    pair_half = lax.broadcasted_iota(jnp.int32, (16, contacts), 0) // 8
    block_ids = []
    for end in range(2):
        body = bodies_ref[end : end + 1, :]
        block = body // lanes
        block_ids.append(block - pair_half)
        hot = jnp.where(lane_ids == body - block * lanes, 1.0, 0.0).astype(BF16)
        onehot[0:lanes, end * contacts : (end + 1) * contacts] = hot
        onehot[lanes : 2 * lanes, end * contacts : (end + 1) * contacts] = hot

    pos_own = jnp.concatenate([pos_ref[...], jnp.zeros((5, lanes), F32)], 0)
    pos_all[me] = pos_own
    for r in range(3):
        target_pos[r] = jnp.broadcast_to(pos_own[r : r + 1, :], (lanes, lanes)).T

    pl.semaphore_wait(barrier, chips)
    gather_start(pos_all, 0, 3)

    current = now_ref[...]
    shifted = current + MOMENTUM * (current - prev_ref[...])

    def first_block(step, parity):
        per_plane = tgt_count // 2
        there = step // per_plane
        return (2 * there + parity) * tgt_count + 2 * lax.rem(step, per_plane)

    for k in range(ITERS):
        phase_sum, phase_force, phase_vel = 1 + 3 * k, 2 + 3 * k, 3 + 3 * k

        pieces = []
        for end in range(2):
            value = rows[end] * shifted
            high = value.astype(BF16).astype(F32)
            low = value - high
            pieces.append(
                (jnp.concatenate([high, high], 0), jnp.concatenate([low, low], 0))
            )

        def scatter(parity):
            def lay_out(step, carry):
                inner = pl.multiple_of(step * 16, 16)
                for end in range(2):
                    here = block_ids[end] == first_block(step, parity)
                    for half in range(2):
                        spread[
                            half, pl.ds(inner, 16), end * contacts : (end + 1) * contacts
                        ] = jnp.where(here, pieces[end][half], 0.0).astype(BF16)
                return carry

            lax.fori_loop(0, chips // 2, lay_out, 0)
            both = lax.dot_general(
                spread[...].reshape(2 * chips * 8, 2 * contacts),
                onehot[0:lanes, :],
                (((1,), (1,)), ((), ())),
                preferred_element_type=F32,
            )
            return (both[: chips * 8] + both[chips * 8 :]).reshape(chips, 8, lanes)

        part[k] = scatter(1 - core)
        start_copy(part.at[k], from_twin.at[k], phase_sum, 0, twin, 1)
        if k == 0:
            gather_own(pos_all, 0, 3, 0)

            def pass_on(i, carry):
                gather_own(pos_all, 0, 3, i)
                return carry

            lax.fori_loop(1, planes, pass_on, 0)
        mine = scatter(core)
        wait_for(from_twin.at[k], recv_sem.at[phase_sum, 0])
        summed[k] = mine + from_twin[k]
        chip = plane * tgt_count + tgt
        for_peers(
            lambda there, column: start_copy(
                summed.at[k, there * tgt_count + column, pl.ds(0, 6)],
                arrived.at[k, chip, pl.ds(0, 6)],
                phase_sum,
                1,
                (2 * there + core, column),
            )
        )
        arrived[k, chip] = summed[k, chip]

        if k == 0:
            def from_the_twin(i, carry):
                gather_twin(pos_all, 0, i)
                return carry

            lax.fori_loop(0, planes, from_the_twin, 0)

            def coefficients(step, carry):
                block = step // (lanes // GROUP)
                group = pl.ds(
                    pl.multiple_of(lax.rem(step, lanes // GROUP) * GROUP, GROUP), GROUP
                )
                dist_sq = None
                for r in range(3):
                    delta = target_pos[r, group, :] - pos_all[block, r : r + 1, :]
                    dist_sq = delta * delta if r == 0 else dist_sq + delta * delta
                inverse = lax.rsqrt(dist_sq)
                inverse_sq = inverse * inverse
                c_one = 0.75 * inverse
                gamma = c_one * inverse_sq
                scaled = gamma * inverse_sq
                coef[block, 0, group, :] = c_one + gamma * (2.0 / 3.0)
                coef[block, 1, group, :] = gamma - 2.0 * scaled
                coef[block, 2, group, :] = gamma
                coef[block, 3, group, :] = 1.5 * scaled
                return carry

            lax.fori_loop(0, 2 * chips * (lanes // GROUP), coefficients, 0, unroll=2)
            diagonal = lax.broadcasted_iota(
                jnp.int32, (lanes, lanes), 0
            ) == lax.broadcasted_iota(jnp.int32, (lanes, lanes), 1)
            for c in range(4):
                coef[me, c] = jnp.where(diagonal, 0.0, coef[me, c])

        wait_for(
            arrived.at[k, pl.ds(0, chips - 1), pl.ds(0, 6)], recv_sem.at[phase_sum, 1]
        )
        own_force = jnp.sum(arrived[k, :, 0:6], 0)
        force_all[k, me, 0:6] = own_force
        forces = force_all.at[k]
        gather_start(forces, phase_force, 6)

        def add_pairs(chunk_id, first):
            def target_group(step, carry):
                group = pl.ds(pl.multiple_of(step * GROUP, GROUP), GROUP)
                where = [target_pos[r, group, :] for r in range(3)]
                if first:
                    sums = [jnp.zeros((GROUP, lanes), F32)] * 6
                else:
                    sums = [total[r, group, :] for r in range(6)]
                for j in range(tgt_count):
                    block = chunk_id * tgt_count + j
                    x, y, z = [where[r] - pos_all[block, r : r + 1, :] for r in range(3)]
                    f_x, f_y, f_z, t_x, t_y, t_z = [
                        force_all[k, block, r : r + 1, :] for r in range(6)
                    ]
                    alpha, beta, gamma, delta = [coef[block, c, group, :] for c in range(4)]
                    along_force = beta * (x * f_x + y * f_y + z * f_z)
                    along_torque = delta * (x * t_x + y * t_y + z * t_z)
                    sums = [
                        sums[0] + (alpha * f_x + along_force * x + gamma * (t_y * z - t_z * y)),
                        sums[1] + (alpha * f_y + along_force * y + gamma * (t_z * x - t_x * z)),
                        sums[2] + (alpha * f_z + along_force * z + gamma * (t_x * y - t_y * x)),
                        sums[3] + (along_torque * x + gamma * (f_y * z - f_z * y - 0.5 * t_x)),
                        sums[4] + (along_torque * y + gamma * (f_z * x - f_x * z - 0.5 * t_y)),
                        sums[5] + (along_torque * z + gamma * (f_x * y - f_y * x - 0.5 * t_z)),
                    ]
                for r in range(6):
                    total[r, group, :] = sums[r]
                return carry

            lax.fori_loop(0, lanes // GROUP, target_group, 0)

        add_pairs(gather_own(forces, phase_force, 6, 0), True)

        def peers_chunk(i, carry):
            add_pairs(gather_own(forces, phase_force, 6, i), False)
            return carry

        def twins_chunk(i, carry):
            add_pairs(gather_twin(forces, phase_force, i), False)
            return carry

        lax.fori_loop(1, planes, peers_chunk, 0)
        lax.fori_loop(0, planes, twins_chunk, 0)

        own_velocity = jnp.concatenate(
            [jnp.sum(total[r].T, 0, keepdims=True) for r in range(6)], 0
        )
        row_ids = lax.broadcasted_iota(jnp.int32, (6, lanes), 0)
        own_velocity = own_velocity + jnp.where(row_ids < 3, 1.0, 0.75) * own_force
        vel_all[k, me, 0:6] = own_velocity
        velocities = vel_all.at[k]
        gather_start(velocities, phase_vel, 6)

        def pick_half(parity, ends):
            blocks = [
                vel_all[k, pl.ds((2 * p + parity) * tgt_count, tgt_count)]
                for p in range(planes)
            ]
            high, low = halves(jnp.concatenate(blocks, 0).reshape(chips * 8, lanes))
            picked[...] = jnp.dot(
                jnp.concatenate([high, low], 1), onehot[...], preferred_element_type=F32
            )

            def pick(step, sums):
                inner = pl.multiple_of(step * 16, 16)
                return tuple(
                    sums[end]
                    + jnp.where(
                        block_ids[end] == first_block(step, parity),
                        picked[pl.ds(inner, 16), end * contacts : (end + 1) * contacts],
                        0.0,
                    )
                    for end in range(2)
                )

            return lax.fori_loop(0, chips // 2, pick, ends)

        gather_own(velocities, phase_vel, 6, 0)

        def pass_velocity(i, carry):
            gather_own(velocities, phase_vel, 6, i)
            return carry

        def take_velocity(i, carry):
            gather_twin(velocities, phase_vel, i)
            return carry

        lax.fori_loop(1, planes, pass_velocity, 0)
        zero = jnp.zeros((16, contacts), F32)
        ends = pick_half(core, (zero, zero))
        lax.fori_loop(0, planes, take_velocity, 0)
        ends = pick_half(1 - core, ends)
        rate = sum(rows[end] * (ends[end][0:8] + ends[end][8:16]) for end in range(2))
        normal_rate = jnp.sum(rate, 0, keepdims=True)
        updated = jnp.maximum(shifted - step_ref[k] * (gaps_ref[...] + normal_rate), 0.0)
        shifted = updated + MOMENTUM * (updated - current)
        current = updated

    result_ref[0:6, :] = own_velocity
    result_ref[6:8, :] = jnp.zeros((2, lanes), F32)
    result_ref[8:, :] = current.reshape(contacts // lanes, lanes)

    gather_sent(pos_all, 0, 3)
    for k in range(ITERS):
        wait_for(part.at[k], send_sem.at[1 + 3 * k, 1])
        wait_for(arrived.at[k, pl.ds(0, chips - 1), pl.ds(0, 6)], send_sem.at[1 + 3 * k, 0])
        gather_sent(force_all.at[k], 2 + 3 * k, 6)
        gather_sent(vel_all.at[k], 3 + 3 * k, 6)


def per_device(
    positions, contact_bodies, contact_frame, gaps, impulse_now, impulse_prev, step_sizes
):
    src_count = lax.axis_size("src")
    tgt_count = lax.axis_size("tgt")
    n = src_count * tgt_count
    lanes = positions.shape[1]
    contacts = gaps.shape[0]
    vmem = pl.BlockSpec(memory_space=pltpu.VMEM)
    result = pl.pallas_call(
        functools.partial(kernel, src_count, tgt_count),
        out_shape=jax.ShapeDtypeStruct((8 + contacts // lanes, lanes), F32),
        in_specs=[vmem] * 6 + [pl.BlockSpec(memory_space=pltpu.SMEM)],
        out_specs=vmem,
        scratch_shapes=[
            pltpu.VMEM((n, 8, lanes), F32),
            pltpu.VMEM((ITERS, n // 2, 8, lanes), F32),
            pltpu.VMEM((ITERS, n // 2, 8, lanes), F32),
            pltpu.VMEM((ITERS, n // 2, 8, lanes), F32),
            pltpu.VMEM((ITERS, n // 2, 8, lanes), F32),
            pltpu.VMEM((ITERS, n, 8, lanes), F32),
            pltpu.VMEM((ITERS, n, 8, lanes), F32),
            pltpu.VMEM((3, lanes, lanes), F32),
            pltpu.VMEM((n, 4, lanes, lanes), F32),
            pltpu.VMEM((6, lanes, lanes), F32),
            pltpu.VMEM((2, n * 4, 2 * contacts), BF16),
            pltpu.VMEM((2 * lanes, 2 * contacts), BF16),
            pltpu.VMEM((n * 4, 2 * contacts), F32),
            pltpu.SemaphoreType.DMA((1 + 3 * ITERS, 2)),
            pltpu.SemaphoreType.DMA((1 + 3 * ITERS, src_count)),
        ],
        compiler_params=pltpu.CompilerParams(
            collective_id=0, has_side_effects=True, vmem_limit_bytes=60 * 1024 * 1024
        ),
    )(
        positions,
        contact_bodies,
        contact_frame,
        gaps.reshape(1, contacts),
        impulse_now.reshape(1, contacts),
        impulse_prev.reshape(1, contacts),
        step_sizes,
    )
    return result[8:].reshape(contacts), result[0:6]


def solution(mesh):
    placed = (
        P(None, ("src", "tgt")),
        P(None, ("src", "tgt")),
        P(None, ("src", "tgt")),
        P(("src", "tgt")),
        P(("src", "tgt")),
        P(("src", "tgt")),
        P(),
    )
    return jax.shard_map(
        per_device,
        mesh=mesh,
        in_specs=placed,
        out_specs=(P(("src", "tgt")), P(None, ("src", "tgt"))),
        check_vma=False,
    )
```

time: 63.2 us -> 58.2 us (0.921)
  Pallas kernels: 60.4 us -> 55.3 us
    pallas_call x1, Pallas kernels: 60.4 us -> 55.3 us  [per_device(): pl.pallas_call(functools.partial(kernel, src_count, tgt_count), out_shape...]
    unnamed x6 -> x2, local copies, waits for them, and re-layouts: 1.94 us -> 0.01 us
    slice x0 -> x1, local copies, waits for them, and re-layouts: none -> 1.33 us  [per_device(): return (result[8:].reshape(contacts), result[0:6])]
where the time goes in v2:
time: 58.2 us; the launch traced here: 57.9 us
  Pallas kernels  55.3 us (95%)
  local copies, waits for them, and re-layouts  1.93 us (3%)
  between operations  0.65 us (1%)
    pallas_call x1, Pallas kernels, per_device(): pl.pallas_call(functools.partial(kernel, src_count, tgt_count), out_shape...  55.3 us
    slice x1, local copies, waits for them, and re-layouts, per_device(): return (result[8:].reshape(contacts), result[0:6])  1.33 us

profile of v2, /device:TPU:0, one launch (start us, length us, event | category | flops | bytes accessed | tf_op | source)
XLA Modules:
  0.0 57.9 jit_solution(7602196585315315901)
XLA Ops:
  0.6 55.3 %shard_map.86 = f32[16,128]{1,0:T(8,128)} custom-call(f32[3,128]{1,0:T(4,128)} %pos_ref.1, s32[2,1024]{1,0:T(2,128)} %bodies_ref.1, f32[9,1024]{1,0:T(8,128)} %frame_ref.1, f32[1,1024]{1,0:T(1,128)} %bitcast.5, f32[1,1024]{1,0:T(1,128)} %bitcast.6, f32[1,1024]{1,0:T(1,128)} %bitcast.7, f32[2]{0:T(128)} %step_ref.1), custom_call_target="tpu_custom_call" | custom-call | tf_op jit(solution)/shard_map/pallas_call | solution.py:391
  56.0 0.0 copy-start
  56.0 1.3 %slice.7 = f32[6,128]{1,0:T(8,128)} slice(f32[16,128]{1,0:T(8,128)} %shard_map.86), slice={[0:6], [0:128]} | slice | bytes 6144 | tf_op jit(solution)/shard_map/slice | solution.py:425
  57.3 0.0 copy-done
  57.3 0.6 %slice_bitcast_fusion = f32[1024]{0:T(1024)} fusion(f32[16,128]{1,0:T(8,128)S(1)} %copy-done), kind=kLoop, calls=%fused_computation | loop fusion | bytes 8192 | tf_op jit(solution)/shard_map/reshape | solution.py:425
Async XLA Ops:
  56.0 1.3 %copy-start = (f32[16,128]{1,0:T(8,128)S(1)}, f32[16,128]{1,0:T(8,128)}, u32[]{:S(2)}) copy-start(f32[16,128]{1,0:T(8,128)} %shard_map.86) | copy-start | bytes 24580
